TPU v7x, 32 devices: a whole 2x2x4 slice. The times are simulated.
32 devices in a mesh: parts: 2 (over y), row: 8 (over z, x), rep: 2 (over core).
Axes of the slice: x: 2, y: 2, z: 4, core: 2. Of those that a mesh axis runs over, the one named last changes fastest.
Arguments:
- features: bfloat16 [4096, 128], P(('parts', 'row')), parts along dimension 0, may hold values from -6 to 6
- tile_values: bfloat16 [16384, 4096], P(('parts', 'row', 'rep')), parts along dimension 0, may hold values from 0 to 1, as said below
- tile_cols: int32 [16384], P(('parts', 'row', 'rep')), parts along dimension 0, may hold values from 0 to 31, as said below
- tile_rows: int32 [16384], P(('parts', 'row', 'rep')), parts along dimension 0, may hold values from 0 to 1
- tile_count: int32 [32], P(('parts', 'row', 'rep')), parts along dimension 0, may hold values from 128 to 512, as said below
- labels: int32 [4096], P(('parts', 'row', 'rep')), parts along dimension 0, may hold values from 0 to 171
- w_self: bfloat16 [128, 256], replicated, may hold values from -0.5 to 0.5
- w_neigh: bfloat16 [128, 256], replicated, may hold values from -0.5 to 0.5
- w_out: bfloat16 [256, 172], replicated
Outputs:
- hidden: bfloat16 [4096, 256], P(('parts', 'row', 'rep')), parts along dimension 0
- grad_self: float32 [256, 256], P(('parts', 'rep')), parts along dimension 0
- grad_neigh: float32 [256, 256], P(('parts', 'rep')), parts along dimension 0
- grad_out: float32 [512, 172], P(('parts', 'rep')), parts along dimension 0
There are 2 independent parts, one for each index of `parts`. A program takes and returns all parts, laid end to end along the dimension named above; an argument that names none is the same for every part. Nothing has to cross between parts.
Inputs may be any that keep to these rules, and one draw needn't show every extreme that they name: `tile_cols`: slot t < 2 of device d is its own diagonal tile: destination tile t, source tile d * 2 + t. Other slots may repeat places. `tile_count`: live slots come first in a device's list; some device has all 512 live. `tile_values`: most entries of a tile are zero; every nonzero is at least 0.05. The diagonal entries of a device's own diagonal tiles are nonzero.
All inputs are finite; a program needn't handle non-finite values.
Results may differ from a plain program's by a relative error of at most 0.001.
The roundings to bfloat16 on the way count: a program that leaves them out, or rounds other values in their place, can miss the bound.
Values may be sent and summed in bfloat16 or wider, within the bound.
A program may use at most 64 MiB of HBM per device.

v0:
```python
import math

import jax
import jax.numpy as jnp
from jax import lax
from jax.sharding import PartitionSpec as P

F = 128
HID = 256
C = 172
TB = 64


step_slots = 64


def aggregate(blocks_all, values, src_cols, dst_rows, live_count, rows_dev):
    slot_total = values.shape[0]
    dst_tiles = rows_dev // TB
    is_live = jnp.arange(slot_total) < live_count
    chosen = ((dst_rows[:, None] == jnp.arange(dst_tiles)[None, :]) & is_live[:, None]).astype(
        jnp.float32
    )
    turns = slot_total // step_slots
    tile_set = values.reshape(turns, step_slots, TB, TB)
    col_sets = src_cols.reshape(turns, step_slots)
    sel_sets = chosen.reshape(turns, step_slots, dst_tiles)

    def one_block(carry, pieces):
        tile_blk, col_blk, sel_blk = pieces
        gathered = blocks_all[col_blk]
        product = jnp.einsum("sij,sjf->sif", tile_blk, gathered, preferred_element_type=jnp.float32)
        total = carry[0] + jnp.einsum(
            "st,sif->tif", sel_blk, product, precision=lax.Precision.HIGHEST
        )
        row_sums = jnp.sum(tile_blk.astype(jnp.float32), axis=2)
        degree = carry[1] + jnp.einsum(
            "st,si->ti", sel_blk, row_sums, precision=lax.Precision.HIGHEST
        )
        return ((total, degree), None)

    start = (jnp.zeros((dst_tiles, TB, F), jnp.float32), jnp.zeros((dst_tiles, TB), jnp.float32))
    (total, degree), _ = lax.scan(one_block, start, (tile_set, col_sets, sel_sets))
    averaged = total / degree[:, :, None]
    return averaged.reshape(dst_tiles * TB, F).astype(jnp.bfloat16)


def local(features, tile_values, tile_cols, tile_rows, tile_count, labels, w_self, w_neigh, w_out):
    rows_dev = labels.shape[0]
    n_row = lax.axis_size("row")
    n_rep = lax.axis_size("rep")
    rep_index = lax.axis_index("rep")
    own_rows = lax.dynamic_slice_in_dim(features, rep_index * rows_dev, rows_dev, 0)
    whole = lax.all_gather(features, "row", axis=0, tiled=True)
    blocks_all = whole.reshape(whole.shape[0] // TB, TB, F)
    neigh = aggregate(blocks_all, tile_values, tile_cols, tile_rows, tile_count[0], rows_dev)
    pre_act = jnp.dot(own_rows, w_self, preferred_element_type=jnp.float32) + jnp.dot(
        neigh, w_neigh, preferred_element_type=jnp.float32
    )
    hidden = jnp.maximum(pre_act, 0.0).astype(jnp.bfloat16)
    logits = jnp.dot(hidden, w_out, preferred_element_type=jnp.float32)
    row_max = jnp.max(logits, axis=1, keepdims=True)
    expo = jnp.exp(logits - row_max)
    probability = expo / jnp.sum(expo, axis=1, keepdims=True)
    one_hot = (labels[:, None] == jnp.arange(C)[None, :]).astype(jnp.float32)
    factor = 1.0 / math.sqrt(rows_dev * n_row * n_rep)
    d_logits = ((probability - one_hot) * factor).astype(jnp.bfloat16)
    part_out = jnp.dot(hidden.T, d_logits, preferred_element_type=jnp.float32)
    back = jnp.dot(d_logits, w_out.T, preferred_element_type=jnp.float32)
    d_pre = jnp.where(pre_act > 0.0, back, 0.0).astype(jnp.bfloat16)
    part_self = jnp.dot(own_rows.T, d_pre, preferred_element_type=jnp.float32)
    part_neigh = jnp.dot(neigh.T, d_pre, preferred_element_type=jnp.float32)
    summed = lax.psum((part_self, part_neigh, part_out), ("row", "rep"))
    feat_rows = F // n_rep
    hid_rows = HID // n_rep
    grad_self = lax.dynamic_slice_in_dim(summed[0], rep_index * feat_rows, feat_rows, 0)
    grad_neigh = lax.dynamic_slice_in_dim(summed[1], rep_index * feat_rows, feat_rows, 0)
    grad_out = lax.dynamic_slice_in_dim(summed[2], rep_index * hid_rows, hid_rows, 0)
    return (hidden, grad_self, grad_neigh, grad_out)


def solution(mesh):
    placed = (
        P(("parts", "row"), None),
        P(("parts", "row", "rep"), None),
        P(("parts", "row", "rep")),
        P(("parts", "row", "rep")),
        P(("parts", "row", "rep")),
        P(("parts", "row", "rep")),
        P(),
        P(),
        P(),
    )
    return jax.shard_map(
        local,
        mesh=mesh,
        in_specs=placed,
        out_specs=(
            P(("parts", "row", "rep"), None),
            P(("parts", "rep"), None),
            P(("parts", "rep"), None),
            P(("parts", "rep"), None),
        ),
        check_vma=False,
    )
```

profile of v0, /device:TPU:0, one launch (start us, length us, event | category | flops | bytes accessed | tf_op | source)
XLA Modules:
  0.0 224.7 jit_solution(11670605221280617601)
XLA Ops:
  7.2 0.0 copy-start
  7.2 0.0 all-reduce.3.cloned.1.call-start
  7.3 0.0 copy-start.1
  7.3 0.0 copy-start.6
  7.3 12.6 %reshape.70 = bf16[8,64,64,64]{3,2,1,0:T(8,128)(2,1)} reshape(bf16[512,4096]{1,0:T(8,128)(2,1)} %param.12) | data formatting | bytes 8388608 | tf_op jit(solution)/shard_map/reshape | solution.py:25
  19.9 35.2 %all_gather.3 = bf16[2048,128]{1,0:T(8,128)(2,1)} all-gather(bf16[256,128]{1,0:T(8,128)(2,1)S(1)} %copy-done.1), channel_id=1, replica_groups=mesh['parts'=2,'row'=8,'rep'=2] {'row'}, dimensions={0}, use_global_device_ids=true | all-gather | bytes 589824 | tf_op jit(solution)/shard_map/all_gather | solution.py:54
  55.1 0.1 eq.29
  55.9 0.1 reshape.71
  56.0 0.0 copy-start.3
  56.0 63.7 %while.13 = (s32[]{:T(128)}, f32[2,64,128]{2,0,1:T(2,128)S(1)}, f32[2,64]{1,0:T(2,128)S(1)}, f32[8,64,2]{1,2,0:T(2,128)S(1)}, bf16[8,64,64,64]{3,2,1,0:T(8,128)(...) while((s32[]{:T(128)}, f32[2,64,128]{2,0,1:T(2,128)S(1)}, ...), condition=%wide.region_2.3_spmd.clone, body=%wide.region_0.2_spmd.clone.sunk | while | flops 80344512 | bytes 9102456 | solution.py:43
  56.0 1.8 gather_fusion
  57.8 1.7 fusion.53
  59.5 2.5 %fusion.54 = f32[2,64,128]{2,0,1:T(2,128)S(1)} fusion(f32[64,64,128]{2,1,0:T(8,128)S(1)} %fusion.53, f32[2,64,128]{2,0,1:T(2,128)S(1)} %get-tuple-element.144, pred[]{:T(512)S(6)} %compare.3, f32[8,64,2]{1,2,0:T(2,128)S(1)} %get-tuple-element.155, s32[]{:T(128)} %get-tuple-element.143), kind=kOutput, calls=%fused_computation.4.clone.1 | convolution fusion | flops 12615680 | bytes 2229253 | tf_op jit(solution)/shard_map/while/body/eval_jaxpr/st,sif->tif/dot_general | solution.py:33
  62.0 1.8 convert_reduce_fusion.2
  63.8 0.1 convolution_add_fusion.3
  64.0 1.8 gather_fusion
  65.8 1.7 fusion.53
  67.5 2.5 %fusion.54 = f32[2,64,128]{2,0,1:T(2,128)S(1)} fusion(f32[64,64,128]{2,1,0:T(8,128)S(1)} %fusion.53, f32[2,64,128]{2,0,1:T(2,128)S(1)} %get-tuple-element.144, pred[]{:T(512)S(6)} %compare.3, f32[8,64,2]{1,2,0:T(2,128)S(1)} %get-tuple-element.155, s32[]{:T(128)} %get-tuple-element.143), kind=kOutput, calls=%fused_computation.4.clone.1 | convolution fusion | flops 12615680 | bytes 2229253 | tf_op jit(solution)/shard_map/while/body/eval_jaxpr/st,sif->tif/dot_general | solution.py:33
  69.9 1.8 convert_reduce_fusion.2
  71.8 0.1 convolution_add_fusion.3
  72.0 1.8 gather_fusion
  73.8 1.7 fusion.53
  75.4 2.5 %fusion.54 = f32[2,64,128]{2,0,1:T(2,128)S(1)} fusion(f32[64,64,128]{2,1,0:T(8,128)S(1)} %fusion.53, f32[2,64,128]{2,0,1:T(2,128)S(1)} %get-tuple-element.144, pred[]{:T(512)S(6)} %compare.3, f32[8,64,2]{1,2,0:T(2,128)S(1)} %get-tuple-element.155, s32[]{:T(128)} %get-tuple-element.143), kind=kOutput, calls=%fused_computation.4.clone.1 | convolution fusion | flops 12615680 | bytes 2229253 | tf_op jit(solution)/shard_map/while/body/eval_jaxpr/st,sif->tif/dot_general | solution.py:33
  77.9 1.8 convert_reduce_fusion.2
  79.7 0.1 convolution_add_fusion.3
  79.9 1.8 gather_fusion
  81.7 1.7 fusion.53
  83.4 2.5 %fusion.54 = f32[2,64,128]{2,0,1:T(2,128)S(1)} fusion(f32[64,64,128]{2,1,0:T(8,128)S(1)} %fusion.53, f32[2,64,128]{2,0,1:T(2,128)S(1)} %get-tuple-element.144, pred[]{:T(512)S(6)} %compare.3, f32[8,64,2]{1,2,0:T(2,128)S(1)} %get-tuple-element.155, s32[]{:T(128)} %get-tuple-element.143), kind=kOutput, calls=%fused_computation.4.clone.1 | convolution fusion | flops 12615680 | bytes 2229253 | tf_op jit(solution)/shard_map/while/body/eval_jaxpr/st,sif->tif/dot_general | solution.py:33
  85.9 1.8 convert_reduce_fusion.2
  87.7 0.1 convolution_add_fusion.3
  87.9 1.8 gather_fusion
  89.7 1.7 fusion.53
  91.4 2.5 %fusion.54 = f32[2,64,128]{2,0,1:T(2,128)S(1)} fusion(f32[64,64,128]{2,1,0:T(8,128)S(1)} %fusion.53, f32[2,64,128]{2,0,1:T(2,128)S(1)} %get-tuple-element.144, pred[]{:T(512)S(6)} %compare.3, f32[8,64,2]{1,2,0:T(2,128)S(1)} %get-tuple-element.155, s32[]{:T(128)} %get-tuple-element.143), kind=kOutput, calls=%fused_computation.4.clone.1 | convolution fusion | flops 12615680 | bytes 2229253 | tf_op jit(solution)/shard_map/while/body/eval_jaxpr/st,sif->tif/dot_general | solution.py:33
  93.8 1.8 convert_reduce_fusion.2
  95.7 0.1 convolution_add_fusion.3
  95.8 1.8 gather_fusion
  97.6 1.7 fusion.53
  99.3 2.5 %fusion.54 = f32[2,64,128]{2,0,1:T(2,128)S(1)} fusion(f32[64,64,128]{2,1,0:T(8,128)S(1)} %fusion.53, f32[2,64,128]{2,0,1:T(2,128)S(1)} %get-tuple-element.144, pred[]{:T(512)S(6)} %compare.3, f32[8,64,2]{1,2,0:T(2,128)S(1)} %get-tuple-element.155, s32[]{:T(128)} %get-tuple-element.143), kind=kOutput, calls=%fused_computation.4.clone.1 | convolution fusion | flops 12615680 | bytes 2229253 | tf_op jit(solution)/shard_map/while/body/eval_jaxpr/st,sif->tif/dot_general | solution.py:33
  101.8 1.8 convert_reduce_fusion.2
  103.6 0.1 convolution_add_fusion.3
  103.8 1.8 gather_fusion
  105.6 1.7 fusion.53
  107.3 2.5 %fusion.54 = f32[2,64,128]{2,0,1:T(2,128)S(1)} fusion(f32[64,64,128]{2,1,0:T(8,128)S(1)} %fusion.53, f32[2,64,128]{2,0,1:T(2,128)S(1)} %get-tuple-element.144, pred[]{:T(512)S(6)} %compare.3, f32[8,64,2]{1,2,0:T(2,128)S(1)} %get-tuple-element.155, s32[]{:T(128)} %get-tuple-element.143), kind=kOutput, calls=%fused_computation.4.clone.1 | convolution fusion | flops 12615680 | bytes 2229253 | tf_op jit(solution)/shard_map/while/body/eval_jaxpr/st,sif->tif/dot_general | solution.py:33
  109.7 1.8 convert_reduce_fusion.2
  111.6 0.1 convolution_add_fusion.3
  111.7 1.8 gather_fusion
  113.5 1.7 fusion.53
  115.2 2.5 %fusion.54 = f32[2,64,128]{2,0,1:T(2,128)S(1)} fusion(f32[64,64,128]{2,1,0:T(8,128)S(1)} %fusion.53, f32[2,64,128]{2,0,1:T(2,128)S(1)} %get-tuple-element.144, pred[]{:T(512)S(6)} %compare.3, f32[8,64,2]{1,2,0:T(2,128)S(1)} %get-tuple-element.155, s32[]{:T(128)} %get-tuple-element.143), kind=kOutput, calls=%fused_computation.4.clone.1 | convolution fusion | flops 12615680 | bytes 2229253 | tf_op jit(solution)/shard_map/while/body/eval_jaxpr/st,sif->tif/dot_general | solution.py:33
  117.7 1.8 convert_reduce_fusion.2
  119.5 0.1 convolution_add_fusion.3
  119.7 0.1 fusion.18
  119.8 0.1 fusion.15
  119.9 0.2 maximum_convert_fusion
  120.1 0.0 copy-start.2
  120.1 0.2 fusion.23
  120.3 0.1 fusion.14
  120.4 0.8 fusion.22
  121.2 0.2 fusion.13
  121.4 0.8 fusion.24
  122.3 0.8 fusion.16
  123.1 0.0 all-reduce.3.cloned.1.call-update
  123.2 91.6 %all-reduce.3.cloned.1.call-done = (f32[128,256]{1,0:T(8,128)}, f32[128,256]{1,0:T(8,128)}, f32[256,172]{0,1:T(8,128)}) async-done(((f32[128,256]{1,0:T(8,128)}, f32[128,256]{1,0:T(8,128)}, f32[256,172]{0,1:T(8,128)}), (f32[128,256]{1,0:T(8,128)}, f32[128,256]{1,0:T(8,128)}, f32[256,172]{0,1:T(8,128)})) %all-reduce.3.cloned.1.call-update) | async-done | bytes 438288 | tf_op jit(solution)/shard_map/psum | solution.py:73
  214.8 1.5 constant_dynamic-slice_fusion.4
  216.3 1.5 constant_dynamic-slice_fusion.5
  (31 shorter events, 0.2 us)
Async XLA Ops:
  7.2 113.0 %copy-start = (bf16[256,172]{0,1:T(8,128)(2,1)S(1)}, bf16[256,172]{0,1:T(8,128)(2,1)}, u32[]{:S(2)}) copy-start(bf16[256,172]{0,1:T(8,128)(2,1)} %param.19) | copy-start | bytes 264196
  7.2 207.6 %all-reduce.3.cloned.1.call-start = ((), (), s32[]{:S(2)}) async-start(), calls=%async_computation | async-start | bytes 884736 | tf_op jit(solution)/shard_map/psum | solution.py:73
  7.3 12.7 %copy-start.1 = (bf16[256,128]{1,0:T(8,128)(2,1)S(1)}, bf16[256,128]{1,0:T(8,128)(2,1)}, u32[]{:S(2)}) copy-start(bf16[256,128]{1,0:T(8,128)(2,1)} %param.11) | copy-start | bytes 196612
  7.3 47.8 %copy-start.5 = (s32[512]{0:T(512)S(1)}, s32[512]{0:T(512)}, u32[]{:S(2)}) copy-start(s32[512]{0:T(512)} %param.14) | copy-start | bytes 6148
  7.3 48.6 %copy-start.6 = (s32[512]{0:T(512)S(1)}, s32[512]{0:T(512)}, u32[]{:S(2)}) copy-start(s32[512]{0:T(512)} %param.13) | copy-start | bytes 6148
  56.0 63.7 %copy-start.3 = (bf16[128,256]{1,0:T(8,128)(2,1)S(1)}, bf16[128,256]{1,0:T(8,128)(2,1)}, u32[]{:S(2)}) copy-start(bf16[128,256]{1,0:T(8,128)(2,1)} %param.17) | copy-start | bytes 196612
  56.0 64.0 %copy-start.4 = (bf16[128,256]{1,0:T(8,128)(2,1)S(1)}, bf16[128,256]{1,0:T(8,128)(2,1)}, u32[]{:S(2)}) copy-start(bf16[128,256]{1,0:T(8,128)(2,1)} %param.18) | copy-start | bytes 196612
  56.0 64.4 %copy-start.7 = (s32[128]{0:T(128)S(1)}, s32[128]{0:T(128)}, u32[]{:S(2)}) copy-start(s32[128]{0:T(128)} %param.16) | copy-start | bytes 1540
  120.1 97.7 %copy-start.2 = (bf16[128,256]{1,0:T(8,128)(2,1)}, bf16[128,256]{1,0:T(8,128)(2,1)S(1)}, u32[]{:S(2)}) copy-start(bf16[128,256]{1,0:T(8,128)(2,1)S(1)} %get-tuple-element.85) | copy-start | bytes 196612
Sparse Core Ops, SparseCore 0:
  123.3 91.4 all-reduce.2
where the time goes:
time: 226 us; the launch traced here: 225 us
  waiting for transfers between devices  91.6 us (41%)
  matrix products  37.4 us (17%)
  blocking collectives  35.2 us (16%)
  local copies, waits for them, and re-layouts  30.2 us (13%)
  other arithmetic  15 us (7%)
  between operations  14.8 us (7%)
    psum x1, waiting for transfers between devices, local(): summed = lax.psum((part_self, part_neigh, part_out), ('row', 'rep'))  91.6 us
    all_gather x1, blocking collectives, local(): whole = lax.all_gather(features, 'row', axis=0, tiled=True)  35.2 us
    dot_general x8, matrix products, one_block(): jnp.einsum('st,sif->tif', sel_blk, product, precision=lax.Precision.HIGHEST)  19.7 us
    reduce_sum x8, other arithmetic, one_block(): row_sums = jnp.sum(tile_blk.astype(jnp.float32), axis=2)  14.8 us
    gather x8, local copies, waits for them, and re-layouts, one_block(): gathered = blocks_all[col_blk]  14.3 us
    dot_general x8, matrix products, one_block(): jnp.einsum('sij,sjf->sif', tile_blk, gathered, preferred_element_type=jnp...  13.4 us
    reshape x1, local copies, waits for them, and re-layouts, aggregate(): tile_set = values.reshape(turns, step_slots, TB, TB)  12.6 us
  transfers between devices with their start and end apart: 1, of which 1 were waited for; matrix products, arithmetic and copies ran while one was open for 0% of the time, Pallas kernels for 0%

commit v1 on v0

--- a/solution.py
+++ b/solution.py
@@ -1,14 +1,278 @@
+import functools
 import math
 
 import jax
 import jax.numpy as jnp
 from jax import lax
+from jax.experimental import pallas as pl
+from jax.experimental.pallas import tpu as pltpu
 from jax.sharding import PartitionSpec as P
 
 F = 128
 HID = 256
 C = 172
 TB = 64
+LANES = 128
+CHUNKS = 4
+MESH = pl.DeviceIdType.MESH
+
+
+def split_rows(n_row):
+    used = 2 * F // 2 * 2 + -(-C // 8) * 8
+    each = -(-used // (8 * n_row)) * 8
+    return each, each * n_row
+
+
+def fused(
+    n_row, feat, values, cols, rows, count, labels, w_self, w_neigh, w_out,
+    hidden_out, gs_out, gn_out, go_out,
+    vbuf, spread, lhs, whole, order, part, got, held, slots, total,
+    v_sem, ga_send, ga_recv, gb_send, gb_recv, ra_send, ra_recv, rb_send, rb_recv, rc_send, rc_recv,
+):
+    me_part = lax.axis_index("parts")
+    me_row = lax.axis_index("row")
+    me_rep = lax.axis_index("rep")
+    other = 1 - me_rep
+    rows_dev = hidden_out.shape[0]
+    dst_tiles = rows_dev // TB
+    n_col = n_row * 2 * dst_tiles
+    n_slot, tile_size = values.shape
+    wide = tile_size // CHUNKS
+    pairs = tile_size // LANES
+    each = slots.shape[1]
+
+    def peer(step):
+        return lax.rem(me_row + step, n_row)
+
+    def at(row, rep):
+        return (me_part, row, rep)
+
+    loads = [
+        pltpu.make_async_copy(values.at[:, pl.ds(n * wide, wide)], vbuf.at[n], v_sem.at[n])
+        for n in range(CHUNKS)
+    ]
+    for copy in loads:
+        copy.start()
+
+    barrier = pltpu.get_barrier_semaphore()
+    pl.semaphore_signal(barrier, inc=1, device_id=at(me_row, other), device_id_type=MESH)
+    for step in range(1, n_row):
+        pl.semaphore_signal(barrier, inc=1, device_id=at(peer(step), me_rep), device_id_type=MESH)
+    pl.semaphore_wait(barrier, n_row)
+
+    mine = pl.ds(pl.multiple_of(me_rep * rows_dev, rows_dev), rows_dev)
+    across, beside = [], []
+    for step in range(1, n_row):
+        here = pl.ds(pl.multiple_of(me_row * 2 * rows_dev + me_rep * rows_dev, rows_dev), rows_dev)
+        across.append(
+            pltpu.make_async_remote_copy(
+                feat.at[mine, :], whole.at[here, :], ga_send.at[step - 1], ga_recv.at[step - 1],
+                device_id=at(peer(step), me_rep), device_id_type=MESH,
+            )
+        )
+        source = lax.rem(me_row - step + n_row, n_row)
+        came = pl.ds(pl.multiple_of(source * 2 * rows_dev + me_rep * rows_dev, rows_dev), rows_dev)
+        beside.append(
+            pltpu.make_async_remote_copy(
+                whole.at[came, :], whole.at[came, :], gb_send.at[step - 1], gb_recv.at[step - 1],
+                device_id=at(me_row, other), device_id_type=MESH,
+            )
+        )
+    for copy in across:
+        copy.start()
+
+    slot = lax.broadcasted_iota(jnp.int32, (1, n_slot), 1)
+    place = jnp.where(slot < count[0], rows[...] * n_col + cols[...], -1)
+    places = lax.broadcasted_iota(jnp.int32, (dst_tiles * n_col, n_slot), 0)
+    pick = jnp.where(places == place, 1.0, 0.0).astype(jnp.bfloat16)
+    per_chunk = pairs // CHUNKS
+    for n in range(CHUNKS):
+        loads[n].wait()
+        block = jnp.dot(pick, vbuf[n], preferred_element_type=jnp.float32)
+        for k in range(per_chunk):
+            spread[pl.ds(n * per_chunk + k, dst_tiles * n_col, stride=pairs), :] = block[
+                :, k * LANES : (k + 1) * LANES
+            ]
+
+    height = dst_tiles * pairs
+    sums = jnp.zeros((height, LANES), jnp.float32)
+    for c in range(n_col):
+        piece = jnp.concatenate(
+            [spread[pl.ds((t * n_col + c) * pairs, pairs), :] for t in range(dst_tiles)], axis=0
+        )
+        sums = sums + piece
+        high = piece.astype(jnp.bfloat16)
+        low = (piece - high.astype(jnp.float32)).astype(jnp.bfloat16)
+        lhs[0:height, pl.ds(c * LANES, LANES)] = high
+        lhs[height : 2 * height, pl.ds(c * LANES, LANES)] = low
+    degree = (
+        jnp.sum(sums[:, :TB], axis=1, keepdims=True),
+        jnp.sum(sums[:, TB:], axis=1, keepdims=True),
+    )
+
+    own = feat[mine, :]
+    pre_self = jnp.dot(own, w_self[...], preferred_element_type=jnp.float32)
+    own_t = own.astype(jnp.float32).T.astype(jnp.bfloat16)
+    class_at = lax.broadcasted_iota(jnp.int32, (C, rows_dev), 0)
+    one_hot = jnp.where(class_at == labels[...], 1.0, 0.0).T
+
+    zero = jnp.zeros((TB, F), jnp.bfloat16)
+
+    def half(ref, start, row, rep):
+        pieces = []
+        for q in range(dst_tiles):
+            x = ref[pl.ds(pl.multiple_of(start + q * TB, TB), TB), :]
+            pieces.append(jnp.concatenate([x, zero], axis=1))
+            pieces.append(jnp.concatenate([zero, x], axis=1))
+        depth = dst_tiles * LANES
+        left = lhs[:, pl.ds(pl.multiple_of((row * 2 + rep) * depth, depth), depth)]
+        return jnp.dot(left, jnp.concatenate(pieces, axis=0), preferred_element_type=jnp.float32)
+
+    acc = half(feat, 0, me_row, 0) + half(feat, rows_dev, me_row, 1)
+    for step in range(1, n_row):
+        across[step - 1].wait_recv()
+        beside[step - 1].start()
+        source = lax.rem(me_row - step + n_row, n_row)
+        acc = acc + half(whole, source * 2 * rows_dev + me_rep * rows_dev, source, me_rep)
+    for step in range(1, n_row):
+        beside[step - 1].wait_recv()
+        source = lax.rem(me_row - step + n_row, n_row)
+        acc = acc + half(whole, source * 2 * rows_dev + other * rows_dev, source, other)
+    agg = acc[:height] + acc[height:]
+    for b in range(2):
+        order[pl.ds(b, height, stride=2), :] = agg[:, b * F : (b + 1) * F] / degree[b]
+    neigh_f = order[...].astype(jnp.bfloat16).astype(jnp.float32)
+    neigh = neigh_f.astype(jnp.bfloat16)
+
+    pre = pre_self + jnp.dot(neigh, w_neigh[...], preferred_element_type=jnp.float32)
+    hidden = jnp.maximum(pre, 0.0).astype(jnp.bfloat16)
+    hidden_out[...] = hidden
+    logits = jnp.dot(hidden, w_out[...], preferred_element_type=jnp.float32)
+    expo = jnp.exp(logits - jnp.max(logits, axis=1, keepdims=True))
+    probability = expo / jnp.sum(expo, axis=1, keepdims=True)
+    factor = 1.0 / math.sqrt(rows_dev * n_row * 2)
+    d_logits = ((probability - one_hot) * factor).astype(jnp.bfloat16)
+
+    def to_partner(n, first, size):
+        span = pl.ds(first, size)
+        return pltpu.make_async_remote_copy(
+            part.at[other, span, :], got.at[span, :], ra_send.at[n], ra_recv.at[n],
+            device_id=at(me_row, other), device_id_type=MESH,
+        )
+
+    n_feat = F // 2
+    top = 4 * n_feat
+    all_rows = part.shape[1]
+    sent = [to_partner(0, top, all_rows - top), to_partner(1, 0, 2 * n_feat), to_partner(2, 2 * n_feat, 2 * n_feat)]
+    out_t = jnp.dot(
+        d_logits.astype(jnp.float32).T.astype(jnp.bfloat16), hidden, preferred_element_type=jnp.float32
+    )
+    for h in range(2):
+        part[h, top + C // 8 * 8 : all_rows, :] = jnp.zeros((all_rows - top - C // 8 * 8, LANES), jnp.float32)
+        part[h, top : top + C, :] = out_t[:, h * LANES : (h + 1) * LANES]
+    sent[0].start()
+    back = lax.dot_general(
+        d_logits, w_out[...], (((1,), (1,)), ((), ())), preferred_element_type=jnp.float32
+    )
+    d_pre = jnp.where(pre > 0.0, back, 0.0).astype(jnp.bfloat16)
+    for n, left in enumerate((own_t, neigh_f.T.astype(jnp.bfloat16))):
+        grad = jnp.dot(left, d_pre, preferred_element_type=jnp.float32)
+        for h in range(2):
+            for b in range(2):
+                part[h, pl.ds((2 * n + b) * n_feat, n_feat), :] = grad[
+                    h * n_feat : (h + 1) * n_feat, b * LANES : (b + 1) * LANES
+                ]
+        sent[1 + n].start()
+
+    spans = (pl.ds(top, all_rows - top), pl.ds(0, 2 * n_feat), pl.ds(2 * n_feat, 2 * n_feat))
+    for n in range(3):
+        sent[n].wait_recv()
+        held[spans[n], :] = part[me_rep, spans[n], :] + got[spans[n], :]
+    apart = []
+    for step in range(1, n_row):
+        span = pl.ds(pl.multiple_of(peer(step) * each, each), each)
+        apart.append(
+            pltpu.make_async_remote_copy(
+                held.at[span, :], slots.at[step - 1], rb_send.at[step - 1], rb_recv.at[step - 1],
+                device_id=at(peer(step), me_rep), device_id_type=MESH,
+            )
+        )
+        apart[-1].start()
+    own_span = pl.ds(pl.multiple_of(me_row * each, each), each)
+    result = held[own_span, :]
+    for step in range(1, n_row):
+        apart[step - 1].wait_recv()
+        result = result + slots[step - 1]
+    total[own_span, :] = result
+    spreads = []
+    for step in range(1, n_row):
+        spreads.append(
+            pltpu.make_async_remote_copy(
+                total.at[own_span, :], total.at[own_span, :], rc_send.at[step - 1], rc_recv.at[step - 1],
+                device_id=at(peer(step), me_rep), device_id_type=MESH,
+            )
+        )
+        spreads[-1].start()
+    for step in range(1, n_row):
+        source = lax.rem(me_row - step + n_row, n_row)
+        span = pl.ds(pl.multiple_of(source * each, each), each)
+        pltpu.make_async_remote_copy(
+            total.at[span, :], total.at[span, :], rc_send.at[step - 1], rc_recv.at[step - 1],
+            device_id=at(peer(step), me_rep), device_id_type=MESH,
+        ).wait_recv()
+    for n, out in enumerate((gs_out, gn_out)):
+        for b in range(2):
+            out[:, b * LANES : (b + 1) * LANES] = total[pl.ds((2 * n + b) * n_feat, n_feat), :]
+    go_out[...] = total[top : top + C, :].T
+    for copy in across + beside + sent + apart + spreads:
+        copy.wait_send()
+
+
+def local(features, tile_values, tile_cols, tile_rows, tile_count, labels, w_self, w_neigh, w_out):
+    rows_dev = labels.shape[0]
+    n_row = lax.axis_size("row")
+    n_slot, tile_size = tile_values.shape
+    dst_tiles = rows_dev // TB
+    n_col = n_row * 2 * dst_tiles
+    pairs = tile_size // LANES
+    each, all_rows = split_rows(n_row)
+    vmem = pl.BlockSpec(memory_space=pltpu.VMEM)
+    dma = pltpu.SemaphoreType.DMA
+    peers = max(n_row - 1, 1)
+    return pl.pallas_call(
+        functools.partial(fused, n_row),
+        out_shape=(
+            jax.ShapeDtypeStruct((rows_dev, HID), jnp.bfloat16),
+            jax.ShapeDtypeStruct((F // 2, HID), jnp.float32),
+            jax.ShapeDtypeStruct((F // 2, HID), jnp.float32),
+            jax.ShapeDtypeStruct((HID // 2, C), jnp.float32),
+        ),
+        in_specs=[
+            vmem, pl.BlockSpec(memory_space=pl.ANY), vmem, vmem,
+            pl.BlockSpec(memory_space=pltpu.SMEM), vmem, vmem, vmem, vmem,
+        ],
+        out_specs=(vmem,) * 4,
+        scratch_shapes=[
+            pltpu.VMEM((CHUNKS, n_slot, tile_size // CHUNKS), jnp.bfloat16),
+            pltpu.VMEM((dst_tiles * n_col * pairs, LANES), jnp.float32),
+            pltpu.VMEM((2 * dst_tiles * pairs, n_col * LANES), jnp.bfloat16),
+            pltpu.VMEM((n_row * 2 * rows_dev, F), jnp.bfloat16),
+            pltpu.VMEM((rows_dev, F), jnp.float32),
+            pltpu.VMEM((2, all_rows, LANES), jnp.float32),
+            pltpu.VMEM((all_rows, LANES), jnp.float32),
+            pltpu.VMEM((all_rows, LANES), jnp.float32),
+            pltpu.VMEM((peers, each, LANES), jnp.float32),
+            pltpu.VMEM((all_rows, LANES), jnp.float32),
+            dma((CHUNKS,)), dma((peers,)), dma((peers,)), dma((peers,)), dma((peers,)),
+            dma((3,)), dma((3,)), dma((peers,)), dma((peers,)), dma((peers,)), dma((peers,)),
+        ],
+        compiler_params=pltpu.CompilerParams(
+            collective_id=0, has_side_effects=True, vmem_limit_bytes=40 * 2**20
+        ),
+    )(
+        features, tile_values, tile_cols.reshape(1, n_slot), tile_rows.reshape(1, n_slot),
+        tile_count, labels.reshape(1, rows_dev), w_self, w_neigh, w_out,
+    )
 
 
 step_slots = 64
@@ -45,7 +309,7 @@
     return averaged.reshape(dst_tiles * TB, F).astype(jnp.bfloat16)
 
 
-def local(features, tile_values, tile_cols, tile_rows, tile_count, labels, w_self, w_neigh, w_out):
+def local_wide(features, tile_values, tile_cols, tile_rows, tile_count, labels, w_self, w_neigh, w_out):
     rows_dev = labels.shape[0]
     n_row = lax.axis_size("row")
     n_rep = lax.axis_size("rep")
@@ -92,7 +356,7 @@
         P(),
     )
     return jax.shard_map(
-        local,
+        local if mesh.shape["row"] <= 16 else local_wide,
         mesh=mesh,
         in_specs=placed,
         out_specs=(

time: 226 us -> 41.3 us (0.18)
  waiting for transfers between devices: 91.6 us -> 0 us
  matrix products: 37.4 us -> 0 us
  blocking collectives: 35.2 us -> 0 us
  Pallas kernels: 0 us -> 29.3 us
  local copies, waits for them, and re-layouts: 30.2 us -> 10.3 us
  other arithmetic: 15 us -> 0 us
  between operations: 14.8 us -> 1.31 us
    psum x1 -> x0, waiting for transfers between devices: 91.6 us -> none  [local(): summed = lax.psum((part_self, part_neigh, part_out), ('row', 'rep'))]
    dot_general x31 -> x0, matrix products: 37.4 us -> none  [the longest x8 19.7 us: one_block(): jnp.einsum('st,sif->tif', sel_blk, product, precision=lax.Precision.HIGHEST)]
    all_gather x1 -> x0, blocking collectives: 35.2 us -> none  [local(): whole = lax.all_gather(features, 'row', axis=0, tiled=True)]
    pallas_call x0 -> x1, Pallas kernels: none -> 29.3 us  [local(): pl.pallas_call(functools.partial(fused, n_row), out_shape=(jax.ShapeDtype...]
    reduce_sum x9 -> x0, other arithmetic: 14.8 us -> none  [the longest x8 14.8 us: one_block(): row_sums = jnp.sum(tile_blk.astype(jnp.float32), axis=2)]
    gather x8 -> x0, local copies, waits for them, and re-layouts: 14.3 us -> none  [one_block(): gathered = blocks_all[col_blk]]
    reshape x2 -> x0, local copies, waits for them, and re-layouts: 12.7 us -> none  [the longest x1 12.6 us: aggregate(): tile_set = values.reshape(turns, step_slots, TB, TB)]
    unnamed x16 -> x18, local copies, waits for them, and re-layouts: 0.05 us -> 9.59 us
  transfers between devices with their start and end apart: 1 -> 0, of which waited for: 1 -> 0; matrix products, arithmetic and copies ran while one was open for 0% -> 0% of each run, Pallas kernels for 0% -> 0%
where the time goes in v1:
time: 41.3 us; the launch traced here: 40.9 us
  Pallas kernels  29.3 us (71%)
  local copies, waits for them, and re-layouts  10.3 us (25%)
  between operations  1.31 us (3%)
    pallas_call x1, Pallas kernels, local(): pl.pallas_call(functools.partial(fused, n_row), out_shape=(jax.ShapeDtype...  29.3 us
    unnamed x18, local copies, waits for them, and re-layouts  9.59 us

profile of v1, /device:TPU:0, one launch (start us, length us, event | category | flops | bytes accessed | tf_op | source)
XLA Modules:
  0.0 40.9 jit_solution(5339838278654990757)
XLA Ops:
  1.3 1.0 %copy.13.w_out = bf16[256,172]{1,0:T(8,128)(2,1)S(1)} copy(bf16[256,172]{0,1:T(8,128)(2,1)} %param.17) | data formatting | bytes 176128 | tf_op args[8]
  2.3 0.0 copy-start
  2.3 2.2 %copy-done = bf16[512,4096]{1,0:T(8,128)(2,1)S(1)} copy-done((bf16[512,4096]{1,0:T(8,128)(2,1)S(1)}, bf16[512,4096]{1,0:T(8,128)(2,1)}, u32[]{:S(2)}) %copy-start) | copy-done | bytes 4194328
  4.5 0.0 copy-start.1
  4.5 0.8 %copy-done.1 = bf16[256,128]{1,0:T(8,128)(2,1)S(1)} copy-done((bf16[256,128]{1,0:T(8,128)(2,1)S(1)}, bf16[256,128]{1,0:T(8,128)(2,1)}, u32[]{:S(2)}) %copy-start.1) | copy-done | bytes 65560
  5.3 0.0 copy-start.2
  5.3 0.8 %copy-done.2 = bf16[128,256]{1,0:T(8,128)(2,1)S(1)} copy-done((bf16[128,256]{1,0:T(8,128)(2,1)S(1)}, bf16[128,256]{1,0:T(8,128)(2,1)}, u32[]{:S(2)}) %copy-start.2) | copy-done | bytes 65560
  6.1 0.0 copy-start.3
  6.1 0.8 %copy-done.3 = bf16[128,256]{1,0:T(8,128)(2,1)S(1)} copy-done((bf16[128,256]{1,0:T(8,128)(2,1)S(1)}, bf16[128,256]{1,0:T(8,128)(2,1)}, u32[]{:S(2)}) %copy-start.3) | copy-done | bytes 65560
  7.0 0.0 copy-start.4
  7.0 0.7 %copy-done.4 = s32[512]{0:T(512)S(1)} copy-done((s32[512]{0:T(512)S(1)}, s32[512]{0:T(512)}, u32[]{:S(2)}) %copy-start.4) | copy-done | bytes 2072
  7.7 0.0 copy-start.5
  7.7 0.7 %copy-done.5 = s32[512]{0:T(512)S(1)} copy-done((s32[512]{0:T(512)S(1)}, s32[512]{0:T(512)}, u32[]{:S(2)}) %copy-start.5) | copy-done | bytes 2072
  8.3 0.0 copy-start.6
  8.3 0.7 %copy-done.6 = s32[128]{0:T(128)S(1)} copy-done((s32[128]{0:T(128)S(1)}, s32[128]{0:T(128)}, u32[]{:S(2)}) %copy-start.6) | copy-done | bytes 536
  9.0 29.3 %shard_map.120 = (bf16[128,256]{1,0:T(8,128)(2,1)S(1)}, f32[64,256]{1,0:T(8,128)S(1)}, f32[64,256]{1,0:T(8,128)S(1)}, f32[128,172]{1,0:T(8,128)S(1)}) custom-call(bf16[256,128]{1,0:T(8,128)(2,1)S(1)} %copy-done.1, bf16[512,4096]{1,0:T(8,128)(2,1)S(1)} %copy-done, s32[1,512]{1,0:T(1,128)S(1)} %bitcast.3, s32[1,512]{1,0:T(1,128)S(1)} %bitcast.4, ...), custom_call_target="tpu_custom_call" | custom-call | tf_op jit(solution)/shard_map/pallas_call | solution.py:242
  38.3 0.7 %copy.14 = f32[128,172]{0,1:T(8,128)} copy(f32[128,172]{1,0:T(8,128)S(1)} %get-tuple-element.7) | data formatting | bytes 176128 | tf_op jit(solution)/shard_map/pallas_call | solution.py:242
  39.0 0.6 %copy.19 = bf16[128,256]{1,0:T(8,128)(2,1)} copy(bf16[128,256]{1,0:T(8,128)(2,1)S(1)} %get-tuple-element.12) | data formatting | bytes 131072
  39.6 0.6 %copy.20 = f32[64,256]{1,0:T(8,128)} copy(f32[64,256]{1,0:T(8,128)S(1)} %get-tuple-element.13) | data formatting | bytes 131072
  40.3 0.6 %copy.21 = f32[64,256]{1,0:T(8,128)} copy(f32[64,256]{1,0:T(8,128)S(1)} %get-tuple-element.14) | data formatting | bytes 131072
Async XLA Ops:
  2.3 2.2 %copy-start = (bf16[512,4096]{1,0:T(8,128)(2,1)S(1)}, bf16[512,4096]{1,0:T(8,128)(2,1)}, u32[]{:S(2)}) copy-start(bf16[512,4096]{1,0:T(8,128)(2,1)} %values.1) | copy-start | bytes 12582916
  4.5 0.8 %copy-start.1 = (bf16[256,128]{1,0:T(8,128)(2,1)S(1)}, bf16[256,128]{1,0:T(8,128)(2,1)}, u32[]{:S(2)}) copy-start(bf16[256,128]{1,0:T(8,128)(2,1)} %feat.1) | copy-start | bytes 196612
  5.3 0.8 %copy-start.2 = (bf16[128,256]{1,0:T(8,128)(2,1)S(1)}, bf16[128,256]{1,0:T(8,128)(2,1)}, u32[]{:S(2)}) copy-start(bf16[128,256]{1,0:T(8,128)(2,1)} %w_self.1) | copy-start | bytes 196612
  6.1 0.8 %copy-start.3 = (bf16[128,256]{1,0:T(8,128)(2,1)S(1)}, bf16[128,256]{1,0:T(8,128)(2,1)}, u32[]{:S(2)}) copy-start(bf16[128,256]{1,0:T(8,128)(2,1)} %w_neigh.1) | copy-start | bytes 196612
  7.0 0.7 %copy-start.4 = (s32[512]{0:T(512)S(1)}, s32[512]{0:T(512)}, u32[]{:S(2)}) copy-start(s32[512]{0:T(512)} %param.11) | copy-start | bytes 6148
  7.7 0.7 %copy-start.5 = (s32[512]{0:T(512)S(1)}, s32[512]{0:T(512)}, u32[]{:S(2)}) copy-start(s32[512]{0:T(512)} %param.12) | copy-start | bytes 6148
  8.3 0.7 %copy-start.6 = (s32[128]{0:T(128)S(1)}, s32[128]{0:T(128)}, u32[]{:S(2)}) copy-start(s32[128]{0:T(128)} %param.14) | copy-start | bytes 1540

commit v2 on v1

--- a/solution.py
+++ b/solution.py
@@ -24,9 +24,9 @@
 
 
 def fused(
-    n_row, feat, values, cols, rows, count, labels, w_self, w_neigh, w_out,
-    hidden_out, gs_out, gn_out, go_out,
-    vbuf, spread, lhs, whole, order, part, got, held, slots, total,
+    n_row, feat_in, values, cols_in, rows_in, count, labels_in, w_self_in, w_neigh_in, w_out_in,
+    hidden_out, total,
+    feat, cols, rows, labels, w_self, w_neigh, w_out, in_sem, vbuf, spread, lhs, whole, order, part, got, held, slots,
     v_sem, ga_send, ga_recv, gb_send, gb_recv, ra_send, ra_recv, rb_send, rb_recv, rc_send, rc_recv,
 ):
     me_part = lax.axis_index("parts")
@@ -51,7 +51,14 @@
         pltpu.make_async_copy(values.at[:, pl.ds(n * wide, wide)], vbuf.at[n], v_sem.at[n])
         for n in range(CHUNKS)
     ]
-    for copy in loads:
+    inputs = [
+        pltpu.make_async_copy(source, target, in_sem.at[n])
+        for n, (source, target) in enumerate((
+            (feat_in, feat), (cols_in, cols), (rows_in, rows), (labels_in, labels),
+            (w_self_in, w_self), (w_neigh_in, w_neigh), (w_out_in, w_out),
+        ))
+    ]
+    for copy in inputs[:3] + loads + inputs[3:]:
         copy.start()
 
     barrier = pltpu.get_barrier_semaphore()
@@ -78,9 +85,12 @@
                 device_id=at(me_row, other), device_id_type=MESH,
             )
         )
+    inputs[0].wait()
     for copy in across:
         copy.start()
 
+    inputs[1].wait()
+    inputs[2].wait()
     slot = lax.broadcasted_iota(jnp.int32, (1, n_slot), 1)
     place = jnp.where(slot < count[0], rows[...] * n_col + cols[...], -1)
     places = lax.broadcasted_iota(jnp.int32, (dst_tiles * n_col, n_slot), 0)
@@ -110,6 +120,8 @@
         jnp.sum(sums[:, TB:], axis=1, keepdims=True),
     )
 
+    for copy in inputs[3:]:
+        copy.wait()
     own = feat[mine, :]
     pre_self = jnp.dot(own, w_self[...], preferred_element_type=jnp.float32)
     own_t = own.astype(jnp.float32).T.astype(jnp.bfloat16)
@@ -147,7 +159,9 @@
     pre = pre_self + jnp.dot(neigh, w_neigh[...], preferred_element_type=jnp.float32)
     hidden = jnp.maximum(pre, 0.0).astype(jnp.bfloat16)
     hidden_out[...] = hidden
-    logits = jnp.dot(hidden, w_out[...], preferred_element_type=jnp.float32)
+    logits = lax.dot_general(
+        hidden, w_out[...], (((1,), (1,)), ((), ())), preferred_element_type=jnp.float32
+    )
     expo = jnp.exp(logits - jnp.max(logits, axis=1, keepdims=True))
     probability = expo / jnp.sum(expo, axis=1, keepdims=True)
     factor = 1.0 / math.sqrt(rows_dev * n_row * 2)
@@ -171,9 +185,7 @@
         part[h, top + C // 8 * 8 : all_rows, :] = jnp.zeros((all_rows - top - C // 8 * 8, LANES), jnp.float32)
         part[h, top : top + C, :] = out_t[:, h * LANES : (h + 1) * LANES]
     sent[0].start()
-    back = lax.dot_general(
-        d_logits, w_out[...], (((1,), (1,)), ((), ())), preferred_element_type=jnp.float32
-    )
+    back = jnp.dot(d_logits, w_out[...], preferred_element_type=jnp.float32)
     d_pre = jnp.where(pre > 0.0, back, 0.0).astype(jnp.bfloat16)
     for n, left in enumerate((own_t, neigh_f.T.astype(jnp.bfloat16))):
         grad = jnp.dot(left, d_pre, preferred_element_type=jnp.float32)
@@ -220,12 +232,24 @@
             total.at[span, :], total.at[span, :], rc_send.at[step - 1], rc_recv.at[step - 1],
             device_id=at(peer(step), me_rep), device_id_type=MESH,
         ).wait_recv()
+    for copy in across + beside + sent + apart + spreads:
+        copy.wait_send()
+
+
+def deliver(hidden, total, hidden_out, gs_out, gn_out, go_out, sem):
+    n_feat = gs_out.shape[0]
+    copies = [(hidden, hidden_out)]
     for n, out in enumerate((gs_out, gn_out)):
         for b in range(2):
-            out[:, b * LANES : (b + 1) * LANES] = total[pl.ds((2 * n + b) * n_feat, n_feat), :]
-    go_out[...] = total[top : top + C, :].T
-    for copy in across + beside + sent + apart + spreads:
-        copy.wait_send()
+            copies.append((
+                total.at[pl.ds((2 * n + b) * n_feat, n_feat), :], out.at[:, pl.ds(b * LANES, LANES)]
+            ))
+    copies.append((total.at[pl.ds(4 * n_feat, C), :], go_out))
+    moves = [pltpu.make_async_copy(a, b, sem.at[n]) for n, (a, b) in enumerate(copies)]
+    for move in moves:
+        move.start()
+    for move in moves:
+        move.wait()
 
 
 def local(features, tile_values, tile_cols, tile_rows, tile_count, labels, w_self, w_neigh, w_out):
@@ -239,20 +263,24 @@
     vmem = pl.BlockSpec(memory_space=pltpu.VMEM)
     dma = pltpu.SemaphoreType.DMA
     peers = max(n_row - 1, 1)
-    return pl.pallas_call(
+    hbm = pl.BlockSpec(memory_space=pl.ANY)
+    hidden, total = pl.pallas_call(
         functools.partial(fused, n_row),
         out_shape=(
             jax.ShapeDtypeStruct((rows_dev, HID), jnp.bfloat16),
-            jax.ShapeDtypeStruct((F // 2, HID), jnp.float32),
-            jax.ShapeDtypeStruct((F // 2, HID), jnp.float32),
-            jax.ShapeDtypeStruct((HID // 2, C), jnp.float32),
+            jax.ShapeDtypeStruct((all_rows, LANES), jnp.float32),
         ),
-        in_specs=[
-            vmem, pl.BlockSpec(memory_space=pl.ANY), vmem, vmem,
-            pl.BlockSpec(memory_space=pltpu.SMEM), vmem, vmem, vmem, vmem,
-        ],
-        out_specs=(vmem,) * 4,
+        in_specs=[hbm] * 4 + [pl.BlockSpec(memory_space=pltpu.SMEM)] + [hbm] * 4,
+        out_specs=(vmem,) * 2,
         scratch_shapes=[
+            pltpu.VMEM(features.shape, jnp.bfloat16),
+            pltpu.VMEM((1, n_slot), jnp.int32),
+            pltpu.VMEM((1, n_slot), jnp.int32),
+            pltpu.VMEM((1, rows_dev), jnp.int32),
+            pltpu.VMEM((F, HID), jnp.bfloat16),
+            pltpu.VMEM((F, HID), jnp.bfloat16),
+            pltpu.VMEM((C, HID), jnp.bfloat16),
+            dma((7,)),
             pltpu.VMEM((CHUNKS, n_slot, tile_size // CHUNKS), jnp.bfloat16),
             pltpu.VMEM((dst_tiles * n_col * pairs, LANES), jnp.float32),
             pltpu.VMEM((2 * dst_tiles * pairs, n_col * LANES), jnp.bfloat16),
@@ -262,17 +290,30 @@
             pltpu.VMEM((all_rows, LANES), jnp.float32),
             pltpu.VMEM((all_rows, LANES), jnp.float32),
             pltpu.VMEM((peers, each, LANES), jnp.float32),
-            pltpu.VMEM((all_rows, LANES), jnp.float32),
             dma((CHUNKS,)), dma((peers,)), dma((peers,)), dma((peers,)), dma((peers,)),
             dma((3,)), dma((3,)), dma((peers,)), dma((peers,)), dma((peers,)), dma((peers,)),
         ],
         compiler_params=pltpu.CompilerParams(
-            collective_id=0, has_side_effects=True, vmem_limit_bytes=40 * 2**20
+            collective_id=0, has_side_effects=True, vmem_limit_bytes=60 * 2**20
         ),
     )(
         features, tile_values, tile_cols.reshape(1, n_slot), tile_rows.reshape(1, n_slot),
-        tile_count, labels.reshape(1, rows_dev), w_self, w_neigh, w_out,
-    )
+        tile_count, labels.reshape(1, rows_dev), w_self, w_neigh, w_out.T,
+    )
+    hidden, grad_self, grad_neigh, grad_out = pl.pallas_call(
+        deliver,
+        out_shape=(
+            jax.ShapeDtypeStruct((rows_dev, HID), jnp.bfloat16),
+            jax.ShapeDtypeStruct((F // 2, HID), jnp.float32),
+            jax.ShapeDtypeStruct((F // 2, HID), jnp.float32),
+            jax.ShapeDtypeStruct((C, HID // 2), jnp.float32),
+        ),
+        in_specs=[hbm] * 2,
+        out_specs=(hbm,) * 4,
+        scratch_shapes=[dma((6,))],
+        compiler_params=pltpu.CompilerParams(vmem_limit_bytes=60 * 2**20),
+    )(hidden, total)
+    return hidden, grad_self, grad_neigh, grad_out.T
 
 
 step_slots = 64

time: 41.3 us -> 40.4 us (0.978)
  local copies, waits for them, and re-layouts: 10.3 us -> 0 us
  Pallas kernels: 29.3 us -> 38.9 us
    pallas_call x0 -> x1, Pallas kernels: none -> 9.78 us  [local(): pl.pallas_call(deliver, out_shape=(jax.ShapeDtypeStruct((rows_dev, HID),...]
    unnamed x18 -> x0, local copies, waits for them, and re-layouts: 9.59 us -> none
    pallas_call x1 -> x0, local copies, waits for them, and re-layouts: 0.74 us -> none  [local(): pl.pallas_call(functools.partial(fused, n_row), out_shape=(jax.ShapeDtype...]
where the time goes in v2:
time: 40.4 us; the launch traced here: 40.2 us
  Pallas kernels  38.9 us (96%)
  between operations  1.29 us (3%)
    pallas_call x1, Pallas kernels, local(): pl.pallas_call(functools.partial(fused, n_row), out_shape=(jax.ShapeDtype...  29.1 us
    pallas_call x1, Pallas kernels, local(): pl.pallas_call(deliver, out_shape=(jax.ShapeDtypeStruct((rows_dev, HID),...  9.78 us

profile of v2, /device:TPU:0, one launch (start us, length us, event | category | flops | bytes accessed | tf_op | source)
XLA Modules:
  0.0 40.2 jit_solution(2695973605439136220)
XLA Ops:
  1.3 29.1 %shard_map.120 = (bf16[128,256]{1,0:T(8,128)(2,1)}, f32[448,128]{1,0:T(8,128)}) custom-call(bf16[256,128]{1,0:T(8,128)(2,1)} %feat_in.1, bf16[512,4096]{1,0:T(8,128)(2,1)} %values.1, s32[1,512]{1,0:T(1,128)} %bitcast.6, s32[1,512]{1,0:T(1,128)} %bitcast.7, s32[1]{0:T(128)S(6)} %copy.13.count, s32[1,128]{1,0:T(1,128)} %bitcast.8, bf16[128,256]{1,0:T(8,128)(2,1)} %w_self_in.1, ...), custom_call_target="tpu_custom_call" | custom-call | tf_op jit(solution)/shard_map/pallas_call | solution.py:267
  30.4 9.8 %shard_map.121 = (bf16[128,256]{1,0:T(8,128)(2,1)}, f32[64,256]{1,0:T(8,128)}, f32[64,256]{1,0:T(8,128)}, f32[172,128]{1,0:T(8,128)}) custom-call(bf16[128,256]{1,0:T(8,128)(2,1)} %get-tuple-element.10.hidden, f32[448,128]{1,0:T(8,128)} %get-tuple-element.11.total), custom_call_target="tpu_custom_call" | custom-call | tf_op jit(solution)/shard_map/pallas_call | solution.py:303

commit v3 on v2

--- a/solution.py
+++ b/solution.py
@@ -18,15 +18,15 @@
 
 
 def split_rows(n_row):
-    used = 2 * F // 2 * 2 + -(-C // 8) * 8
-    each = -(-used // (8 * n_row)) * 8
-    return each, each * n_row
+    first = 2 * F // n_row
+    last = -(-C // (8 * n_row)) * 8
+    return -(-(first + last + 8) // 16) * 16, (first + last) * n_row
 
 
 def fused(
     n_row, feat_in, values, cols_in, rows_in, count, labels_in, w_self_in, w_neigh_in, w_out_in,
     hidden_out, total,
-    feat, cols, rows, labels, w_self, w_neigh, w_out, in_sem, vbuf, spread, lhs, whole, order, part, got, held, slots,
+    feat, cols, rows, labels, w_self, w_neigh, w_out, in_sem, vbuf, spread, lhs, whole, order, part, got, held, codes, slots, everyone,
     v_sem, ga_send, ga_recv, gb_send, gb_recv, ra_send, ra_recv, rb_send, rb_recv, rc_send, rc_recv,
 ):
     me_part = lax.axis_index("parts")
@@ -39,7 +39,6 @@
     n_slot, tile_size = values.shape
     wide = tile_size // CHUNKS
     pairs = tile_size // LANES
-    each = slots.shape[1]
 
     def peer(step):
         return lax.rem(me_row + step, n_row)
@@ -200,53 +199,92 @@
     for n in range(3):
         sent[n].wait_recv()
         held[spans[n], :] = part[me_rep, spans[n], :] + got[spans[n], :]
+    size = (2 * n_feat // n_row, 2 * n_feat // n_row, (all_rows - top) // n_row)
+    base = (0, 2 * n_feat, top)
+
+    def spans_of(row):
+        return [pl.ds(pl.multiple_of(b + row * n, 8), n) for b, n in zip(base, size)]
+
+    def encode(pieces):
+        powers, whole_code = [], []
+        for x in pieces:
+            peak = jnp.maximum(jnp.max(jnp.abs(x), axis=0, keepdims=True), 1e-34)
+            power = jnp.floor(jnp.log2(peak))
+            powers.append(power)
+            whole_code.append(jnp.floor(x * jnp.exp2(13.0 - power) + 0.5))
+        line = lax.broadcasted_iota(jnp.int32, (8, LANES), 0)
+        whole_code.append(jnp.where(line == 0, powers[0], jnp.where(line == 1, powers[1], powers[2])))
+        spare = slots.shape[1] - sum(size) - 8
+        if spare:
+            whole_code.append(jnp.zeros((spare, LANES), jnp.float32))
+        return jnp.concatenate(whole_code, axis=0).astype(jnp.int32).astype(jnp.int16)
+
+    def decode(code):
+        x = code.astype(jnp.int32).astype(jnp.float32)
+        pieces, first, last = [], 0, sum(size)
+        for n in range(3):
+            pieces.append(x[first : first + size[n]] * jnp.exp2(x[last + n : last + n + 1] - 13.0))
+            first += size[n]
+        return pieces
+
     apart = []
     for step in range(1, n_row):
-        span = pl.ds(pl.multiple_of(peer(step) * each, each), each)
+        codes[step - 1] = encode([held[span, :] for span in spans_of(peer(step))])
         apart.append(
             pltpu.make_async_remote_copy(
-                held.at[span, :], slots.at[step - 1], rb_send.at[step - 1], rb_recv.at[step - 1],
+                codes.at[step - 1], slots.at[step - 1], rb_send.at[step - 1], rb_recv.at[step - 1],
                 device_id=at(peer(step), me_rep), device_id_type=MESH,
             )
         )
         apart[-1].start()
-    own_span = pl.ds(pl.multiple_of(me_row * each, each), each)
-    result = held[own_span, :]
+    result = [held[span, :] for span in spans_of(me_row)]
     for step in range(1, n_row):
         apart[step - 1].wait_recv()
-        result = result + slots[step - 1]
-    total[own_span, :] = result
+        result = [a + b for a, b in zip(result, decode(slots[step - 1]))]
+    everyone[me_row] = encode(result)
     spreads = []
     for step in range(1, n_row):
         spreads.append(
             pltpu.make_async_remote_copy(
-                total.at[own_span, :], total.at[own_span, :], rc_send.at[step - 1], rc_recv.at[step - 1],
+                everyone.at[me_row], everyone.at[me_row], rc_send.at[step - 1], rc_recv.at[step - 1],
                 device_id=at(peer(step), me_rep), device_id_type=MESH,
             )
         )
         spreads[-1].start()
-    for step in range(1, n_row):
+    for step in range(n_row):
         source = lax.rem(me_row - step + n_row, n_row)
-        span = pl.ds(pl.multiple_of(source * each, each), each)
-        pltpu.make_async_remote_copy(
-            total.at[span, :], total.at[span, :], rc_send.at[step - 1], rc_recv.at[step - 1],
-            device_id=at(peer(step), me_rep), device_id_type=MESH,
-        ).wait_recv()
+        if step:
+            pltpu.make_async_remote_copy(
+                everyone.at[source], everyone.at[source], rc_send.at[step - 1], rc_recv.at[step - 1],
+                device_id=at(peer(step), me_rep), device_id_type=MESH,
+            ).wait_recv()
+        for span, x in zip(spans_of(source), decode(everyone[source])):
+            total[span, :] = x
     for copy in across + beside + sent + apart + spreads:
         copy.wait_send()
 
 
-def deliver(hidden, total, hidden_out, gs_out, gn_out, go_out, sem):
+def deliver(hidden, total, hidden_out, gs_out, gn_out, go_out, near_hidden, near_total, in_sem, sem):
+    top = 4 * gs_out.shape[0]
+    cuts = [(hidden, near_hidden)] + [
+        (total.at[a:b, :], near_total.at[a:b, :])
+        for a, b in ((0, top // 2), (top // 2, top), (top, total.shape[0]))
+    ]
+    loads = [pltpu.make_async_copy(a, b, in_sem.at[n]) for n, (a, b) in enumerate(cuts)]
+    for load in loads:
+        load.start()
     n_feat = gs_out.shape[0]
-    copies = [(hidden, hidden_out)]
+    copies = [(near_hidden, hidden_out)]
     for n, out in enumerate((gs_out, gn_out)):
         for b in range(2):
             copies.append((
-                total.at[pl.ds((2 * n + b) * n_feat, n_feat), :], out.at[:, pl.ds(b * LANES, LANES)]
+                near_total.at[pl.ds((2 * n + b) * n_feat, n_feat), :], out.at[:, pl.ds(b * LANES, LANES)]
             ))
-    copies.append((total.at[pl.ds(4 * n_feat, C), :], go_out))
+    copies.append((near_total.at[pl.ds(4 * n_feat, C), :], go_out))
     moves = [pltpu.make_async_copy(a, b, sem.at[n]) for n, (a, b) in enumerate(copies)]
-    for move in moves:
+    for n, move in enumerate(moves):
+        if n in (0, 1, 3, 5):
+            loads[(n + 1) // 2].wait()
         move.start()
     for move in moves:
         move.wait()
@@ -289,7 +327,9 @@
             pltpu.VMEM((2, all_rows, LANES), jnp.float32),
             pltpu.VMEM((all_rows, LANES), jnp.float32),
             pltpu.VMEM((all_rows, LANES), jnp.float32),
-            pltpu.VMEM((peers, each, LANES), jnp.float32),
+            pltpu.VMEM((peers, each, LANES), jnp.int16),
+            pltpu.VMEM((peers, each, LANES), jnp.int16),
+            pltpu.VMEM((n_row, each, LANES), jnp.int16),
             dma((CHUNKS,)), dma((peers,)), dma((peers,)), dma((peers,)), dma((peers,)),
             dma((3,)), dma((3,)), dma((peers,)), dma((peers,)), dma((peers,)), dma((peers,)),
         ],
@@ -310,7 +350,11 @@
         ),
         in_specs=[hbm] * 2,
         out_specs=(hbm,) * 4,
-        scratch_shapes=[dma((6,))],
+        scratch_shapes=[
+            pltpu.VMEM((rows_dev, HID), jnp.bfloat16),
+            pltpu.VMEM((all_rows, LANES), jnp.float32),
+            dma((4,)), dma((6,)),
+        ],
         compiler_params=pltpu.CompilerParams(vmem_limit_bytes=60 * 2**20),
     )(hidden, total)
     return hidden, grad_self, grad_neigh, grad_out.T
@@ -397,7 +441,7 @@
         P(),
     )
     return jax.shard_map(
-        local if mesh.shape["row"] <= 16 else local_wide,
+        local if mesh.shape["row"] in (2, 4, 8) else local_wide,
         mesh=mesh,
         in_specs=placed,
         out_specs=(

time: 40.4 us -> 30 us (0.74)
  Pallas kernels: 38.9 us -> 28.5 us
    pallas_call x1, Pallas kernels: 9.78 us -> 1.72 us  [local(): pl.pallas_call(deliver, out_shape=(jax.ShapeDtypeStruct((rows_dev, HID),...]
    pallas_call x1, Pallas kernels: 29.1 us -> 26.8 us  [local(): pl.pallas_call(functools.partial(fused, n_row), out_shape=(jax.ShapeDtype...]
where the time goes in v3:
time: 30 us; the launch traced here: 29.8 us
  Pallas kernels  28.5 us (95%)
  between operations  1.29 us (4%)
    pallas_call x1, Pallas kernels, local(): pl.pallas_call(functools.partial(fused, n_row), out_shape=(jax.ShapeDtype...  26.8 us
    pallas_call x1, Pallas kernels, local(): pl.pallas_call(deliver, out_shape=(jax.ShapeDtypeStruct((rows_dev, HID),...  1.72 us

profile of v3, /device:TPU:0, one launch (start us, length us, event | category | flops | bytes accessed | tf_op | source)
XLA Modules:
  0.0 29.8 jit_solution(11666292775544415324)
XLA Ops:
  1.3 26.8 %shard_map.120 = (bf16[128,256]{1,0:T(8,128)(2,1)}, f32[448,128]{1,0:T(8,128)}) custom-call(bf16[256,128]{1,0:T(8,128)(2,1)} %feat_in.1, bf16[512,4096]{1,0:T(8,128)(2,1)} %values.1, s32[1,512]{1,0:T(1,128)} %bitcast.6, s32[1,512]{1,0:T(1,128)} %bitcast.7, s32[1]{0:T(128)S(6)} %copy.13.count, s32[1,128]{1,0:T(1,128)} %bitcast.8, bf16[128,256]{1,0:T(8,128)(2,1)} %w_self_in.1, ...), custom_call_target="tpu_custom_call" | custom-call | tf_op jit(solution)/shard_map/pallas_call | solution.py:305
  28.1 1.7 %shard_map.121 = (bf16[128,256]{1,0:T(8,128)(2,1)}, f32[64,256]{1,0:T(8,128)}, f32[64,256]{1,0:T(8,128)}, f32[172,128]{1,0:T(8,128)}) custom-call(bf16[128,256]{1,0:T(8,128)(2,1)} %get-tuple-element.10.hidden, f32[448,128]{1,0:T(8,128)} %get-tuple-element.11.total), custom_call_target="tpu_custom_call" | custom-call | tf_op jit(solution)/shard_map/pallas_call | solution.py:343

commit v4 on v3

--- a/solution.py
+++ b/solution.py
@@ -264,27 +264,17 @@
         copy.wait_send()
 
 
-def deliver(hidden, total, hidden_out, gs_out, gn_out, go_out, near_hidden, near_total, in_sem, sem):
-    top = 4 * gs_out.shape[0]
-    cuts = [(hidden, near_hidden)] + [
-        (total.at[a:b, :], near_total.at[a:b, :])
-        for a, b in ((0, top // 2), (top // 2, top), (top, total.shape[0]))
-    ]
-    loads = [pltpu.make_async_copy(a, b, in_sem.at[n]) for n, (a, b) in enumerate(cuts)]
-    for load in loads:
-        load.start()
+def deliver(hidden, total, hidden_out, gs_out, gn_out, go_out, sem):
     n_feat = gs_out.shape[0]
-    copies = [(near_hidden, hidden_out)]
+    copies = [(hidden, hidden_out)]
     for n, out in enumerate((gs_out, gn_out)):
         for b in range(2):
             copies.append((
-                near_total.at[pl.ds((2 * n + b) * n_feat, n_feat), :], out.at[:, pl.ds(b * LANES, LANES)]
+                total.at[pl.ds((2 * n + b) * n_feat, n_feat), :], out.at[:, pl.ds(b * LANES, LANES)]
             ))
-    copies.append((near_total.at[pl.ds(4 * n_feat, C), :], go_out))
+    copies.append((total.at[pl.ds(4 * n_feat, C), :], go_out))
     moves = [pltpu.make_async_copy(a, b, sem.at[n]) for n, (a, b) in enumerate(copies)]
-    for n, move in enumerate(moves):
-        if n in (0, 1, 3, 5):
-            loads[(n + 1) // 2].wait()
+    for move in moves:
         move.start()
     for move in moves:
         move.wait()
@@ -305,8 +295,8 @@
     hidden, total = pl.pallas_call(
         functools.partial(fused, n_row),
         out_shape=(
-            jax.ShapeDtypeStruct((rows_dev, HID), jnp.bfloat16),
-            jax.ShapeDtypeStruct((all_rows, LANES), jnp.float32),
+            pltpu.VMEM((rows_dev, HID), jnp.bfloat16),
+            pltpu.VMEM((all_rows, LANES), jnp.float32),
         ),
         in_specs=[hbm] * 4 + [pl.BlockSpec(memory_space=pltpu.SMEM)] + [hbm] * 4,
         out_specs=(vmem,) * 2,
@@ -348,14 +338,10 @@
             jax.ShapeDtypeStruct((F // 2, HID), jnp.float32),
             jax.ShapeDtypeStruct((C, HID // 2), jnp.float32),
         ),
-        in_specs=[hbm] * 2,
+        in_specs=[vmem] * 2,
         out_specs=(hbm,) * 4,
-        scratch_shapes=[
-            pltpu.VMEM((rows_dev, HID), jnp.bfloat16),
-            pltpu.VMEM((all_rows, LANES), jnp.float32),
-            dma((4,)), dma((6,)),
-        ],
-        compiler_params=pltpu.CompilerParams(vmem_limit_bytes=60 * 2**20),
+        scratch_shapes=[dma((6,))],
+        compiler_params=pltpu.CompilerParams(vmem_limit_bytes=2**20),
     )(hidden, total)
     return hidden, grad_self, grad_neigh, grad_out.T
 

time: 30 us -> 28.3 us (0.943)
  Pallas kernels: 28.5 us -> 26.9 us
    pallas_call x1, Pallas kernels: 1.72 us -> 0.76 us  [local(): pl.pallas_call(deliver, out_shape=(jax.ShapeDtypeStruct((rows_dev, HID),...]
    pallas_call x1, Pallas kernels: 26.8 us -> 26.1 us  [local(): pl.pallas_call(functools.partial(fused, n_row), out_shape=(pltpu.VMEM((ro...]
where the time goes in v4:
time: 28.3 us; the launch traced here: 28.2 us
  Pallas kernels  26.9 us (95%)
  between operations  1.29 us (5%)
    pallas_call x1, Pallas kernels, local(): pl.pallas_call(functools.partial(fused, n_row), out_shape=(pltpu.VMEM((ro...  26.1 us
    pallas_call x1, Pallas kernels, local(): pl.pallas_call(deliver, out_shape=(jax.ShapeDtypeStruct((rows_dev, HID),...  0.76 us

profile of v4, /device:TPU:0, one launch (start us, length us, event | category | flops | bytes accessed | tf_op | source)
XLA Modules:
  0.0 28.2 jit_solution(8845184646401336041)
XLA Ops:
  1.3 26.1 %shard_map.120 = (bf16[128,256]{1,0:T(8,128)(2,1)S(1)}, f32[448,128]{1,0:T(8,128)S(1)}) custom-call(bf16[256,128]{1,0:T(8,128)(2,1)} %feat_in.1, bf16[512,4096]{1,0:T(8,128)(2,1)} %values.1, s32[1,512]{1,0:T(1,128)} %bitcast.6, s32[1,512]{1,0:T(1,128)} %bitcast.7, s32[1]{0:T(128)S(6)} %copy.13.count, s32[1,128]{1,0:T(1,128)} %bitcast.8, ...), custom_call_target="tpu_custom_call" | custom-call | tf_op jit(solution)/shard_map/pallas_call | solution.py:295
  27.4 0.8 %shard_map.121 = (bf16[128,256]{1,0:T(8,128)(2,1)}, f32[64,256]{1,0:T(8,128)}, f32[64,256]{1,0:T(8,128)}, f32[172,128]{1,0:T(8,128)}) custom-call(bf16[128,256]{1,0:T(8,128)(2,1)S(1)} %get-tuple-element.10.hidden, f32[448,128]{1,0:T(8,128)S(1)} %get-tuple-element.11.total), custom_call_target="tpu_custom_call" | custom-call | tf_op jit(solution)/shard_map/pallas_call | solution.py:333

commit v5 on v4

--- a/solution.py
+++ b/solution.py
@@ -177,6 +177,8 @@
     top = 4 * n_feat
     all_rows = part.shape[1]
     sent = [to_partner(0, top, all_rows - top), to_partner(1, 0, 2 * n_feat), to_partner(2, 2 * n_feat, 2 * n_feat)]
+    back = jnp.dot(d_logits, w_out[...], preferred_element_type=jnp.float32)
+    d_pre = jnp.where(pre > 0.0, back, 0.0).astype(jnp.bfloat16)
     out_t = jnp.dot(
         d_logits.astype(jnp.float32).T.astype(jnp.bfloat16), hidden, preferred_element_type=jnp.float32
     )
@@ -184,8 +186,6 @@
         part[h, top + C // 8 * 8 : all_rows, :] = jnp.zeros((all_rows - top - C // 8 * 8, LANES), jnp.float32)
         part[h, top : top + C, :] = out_t[:, h * LANES : (h + 1) * LANES]
     sent[0].start()
-    back = jnp.dot(d_logits, w_out[...], preferred_element_type=jnp.float32)
-    d_pre = jnp.where(pre > 0.0, back, 0.0).astype(jnp.bfloat16)
     for n, left in enumerate((own_t, neigh_f.T.astype(jnp.bfloat16))):
         grad = jnp.dot(left, d_pre, preferred_element_type=jnp.float32)
         for h in range(2):
@@ -202,46 +202,49 @@
     size = (2 * n_feat // n_row, 2 * n_feat // n_row, (all_rows - top) // n_row)
     base = (0, 2 * n_feat, top)
 
-    def spans_of(row):
-        return [pl.ds(pl.multiple_of(b + row * n, 8), n) for b, n in zip(base, size)]
-
     def encode(pieces):
         powers, whole_code = [], []
         for x in pieces:
-            peak = jnp.maximum(jnp.max(jnp.abs(x), axis=0, keepdims=True), 1e-34)
+            peak = jnp.maximum(jnp.max(jnp.abs(x), axis=1, keepdims=True), 1e-34)
             power = jnp.floor(jnp.log2(peak))
             powers.append(power)
             whole_code.append(jnp.floor(x * jnp.exp2(13.0 - power) + 0.5))
-        line = lax.broadcasted_iota(jnp.int32, (8, LANES), 0)
+        count_of = pieces[0].shape[0]
+        line = lax.broadcasted_iota(jnp.int32, (count_of, 8, LANES), 1)
         whole_code.append(jnp.where(line == 0, powers[0], jnp.where(line == 1, powers[1], powers[2])))
         spare = slots.shape[1] - sum(size) - 8
         if spare:
-            whole_code.append(jnp.zeros((spare, LANES), jnp.float32))
-        return jnp.concatenate(whole_code, axis=0).astype(jnp.int32).astype(jnp.int16)
+            whole_code.append(jnp.zeros((count_of, spare, LANES), jnp.float32))
+        return jnp.concatenate(whole_code, axis=1).astype(jnp.int32).astype(jnp.int16)
 
     def decode(code):
         x = code.astype(jnp.int32).astype(jnp.float32)
         pieces, first, last = [], 0, sum(size)
         for n in range(3):
-            pieces.append(x[first : first + size[n]] * jnp.exp2(x[last + n : last + n + 1] - 13.0))
+            scale = jnp.exp2(x[:, last + n : last + n + 1] - 13.0)
+            pieces.append(x[:, first : first + size[n]] * scale)
             first += size[n]
         return pieces
 
+    codes[...] = encode([
+        held[b : b + n_row * n, :].reshape(n_row, n, LANES) for b, n in zip(base, size)
+    ])
     apart = []
     for step in range(1, n_row):
-        codes[step - 1] = encode([held[span, :] for span in spans_of(peer(step))])
         apart.append(
             pltpu.make_async_remote_copy(
-                codes.at[step - 1], slots.at[step - 1], rb_send.at[step - 1], rb_recv.at[step - 1],
+                codes.at[peer(step)], slots.at[step - 1], rb_send.at[step - 1], rb_recv.at[step - 1],
                 device_id=at(peer(step), me_rep), device_id_type=MESH,
             )
         )
         apart[-1].start()
-    result = [held[span, :] for span in spans_of(me_row)]
-    for step in range(1, n_row):
-        apart[step - 1].wait_recv()
-        result = [a + b for a, b in zip(result, decode(slots[step - 1]))]
-    everyone[me_row] = encode(result)
+    result = [
+        held[pl.ds(pl.multiple_of(b + me_row * n, 8), n), :] for b, n in zip(base, size)
+    ]
+    for copy in apart:
+        copy.wait_recv()
+    result = [a + jnp.sum(b, axis=0) for a, b in zip(result, decode(slots[...]))]
+    everyone[me_row] = encode([x[None] for x in result])[0]
     spreads = []
     for step in range(1, n_row):
         spreads.append(
@@ -251,15 +254,14 @@
             )
         )
         spreads[-1].start()
-    for step in range(n_row):
+    for step in range(1, n_row):
         source = lax.rem(me_row - step + n_row, n_row)
-        if step:
-            pltpu.make_async_remote_copy(
-                everyone.at[source], everyone.at[source], rc_send.at[step - 1], rc_recv.at[step - 1],
-                device_id=at(peer(step), me_rep), device_id_type=MESH,
-            ).wait_recv()
-        for span, x in zip(spans_of(source), decode(everyone[source])):
-            total[span, :] = x
+        pltpu.make_async_remote_copy(
+            everyone.at[source], everyone.at[source], rc_send.at[step - 1], rc_recv.at[step - 1],
+            device_id=at(peer(step), me_rep), device_id_type=MESH,
+        ).wait_recv()
+    for b, n, x in zip(base, size, decode(everyone[...])):
+        total[b : b + n_row * n, :] = x.reshape(n_row * n, LANES)
     for copy in across + beside + sent + apart + spreads:
         copy.wait_send()
 
@@ -317,7 +319,7 @@
             pltpu.VMEM((2, all_rows, LANES), jnp.float32),
             pltpu.VMEM((all_rows, LANES), jnp.float32),
             pltpu.VMEM((all_rows, LANES), jnp.float32),
-            pltpu.VMEM((peers, each, LANES), jnp.int16),
+            pltpu.VMEM((n_row, each, LANES), jnp.int16),
             pltpu.VMEM((peers, each, LANES), jnp.int16),
             pltpu.VMEM((n_row, each, LANES), jnp.int16),
             dma((CHUNKS,)), dma((peers,)), dma((peers,)), dma((peers,)), dma((peers,)),

time: 28.3 us -> 28.1 us (level)
  no operation moved by 1% of the time
where the time goes in v5:
time: 28.1 us; the launch traced here: 28 us
  Pallas kernels  26.7 us (95%)
  between operations  1.29 us (5%)
    pallas_call x1, Pallas kernels, local(): pl.pallas_call(functools.partial(fused, n_row), out_shape=(pltpu.VMEM((ro...  25.9 us
    pallas_call x1, Pallas kernels, local(): pl.pallas_call(deliver, out_shape=(jax.ShapeDtypeStruct((rows_dev, HID),...  0.76 us

profile of v5, /device:TPU:0, one launch (start us, length us, event | category | flops | bytes accessed | tf_op | source)
XLA Modules:
  0.0 28.0 jit_solution(12882999364506085210)
XLA Ops:
  1.3 25.9 %shard_map.120 = (bf16[128,256]{1,0:T(8,128)(2,1)S(1)}, f32[448,128]{1,0:T(8,128)S(1)}) custom-call(bf16[256,128]{1,0:T(8,128)(2,1)} %feat_in.1, bf16[512,4096]{1,0:T(8,128)(2,1)} %values.1, s32[1,512]{1,0:T(1,128)} %bitcast.6, s32[1,512]{1,0:T(1,128)} %bitcast.7, s32[1]{0:T(128)S(6)} %copy.13.count, s32[1,128]{1,0:T(1,128)} %bitcast.8, ...), custom_call_target="tpu_custom_call" | custom-call | tf_op jit(solution)/shard_map/pallas_call | solution.py:297
  27.2 0.8 %shard_map.121 = (bf16[128,256]{1,0:T(8,128)(2,1)}, f32[64,256]{1,0:T(8,128)}, f32[64,256]{1,0:T(8,128)}, f32[172,128]{1,0:T(8,128)}) custom-call(bf16[128,256]{1,0:T(8,128)(2,1)S(1)} %get-tuple-element.10.hidden, f32[448,128]{1,0:T(8,128)S(1)} %get-tuple-element.11.total), custom_call_target="tpu_custom_call" | custom-call | tf_op jit(solution)/shard_map/pallas_call | solution.py:335
